TPU v7x, 512 devices: a whole 4x8x8 slice. The times are simulated.
512 devices in a mesh: gy: 16 (over z_hi, y), gz: 4 (over z_lo), band: 8 (over x, core).
Axes of the slice: x: 4, y: 8, z: 8 (z_hi: 2, z_lo: 4; z = z_hi * 4 + z_lo), core: 2. Of those that a mesh axis runs over, the one named last changes fastest.
Arguments:
- previous: float32 [128, 128, 32, 128], P('band', 'gy', 'gz'), may hold values from -2.4 to 2.4
- current: float32 [128, 128, 32, 128], P('band', 'gy', 'gz'), may hold values from 0.5 to 4.5
- potential: float32 [128, 32, 128], P('gy', 'gz'), may hold values from 0 to 2
- projectors: float32 [64, 128, 32, 128], P(None, 'gy', 'gz'), may hold values from -0.0625 to 0.0625
- couplings: float32 [64], replicated, may hold values from 0.5 to 2
- pattern: int32 [8, 64], replicated, may hold values 0 or 1
- counts: int32 [8], replicated, may hold values from 1 to 8, as said below
- panels: float32 [256, 128, 32, 128], P('band', 'gy', 'gz'), may hold values from -0.03125 to 0.03125
Outputs:
- rotated: float32 [128, 128, 32, 128], P('band', 'gy', 'gz')
- coefficients: float32 [256, 128], P(None, 'band')
Inputs may be any that keep to these rules, and one draw needn't show every extreme that they name: `counts`: some atom block has all 8 slots live.
All inputs are finite; a program needn't handle non-finite values.
Results may differ from a plain program's by a relative error of at most 0.00011.
Values sent between devices are 32-bit elements; how exact they have to be, the bound alone decides.
A program may use at most 128 MiB of HBM per device.

v0:
```python
import jax
import jax.numpy as jnp
from jax import lax
from jax.sharding import PartitionSpec as P

STENCIL = (
    -5369.0 / 1800.0,
    12.0 / 7.0,
    -15.0 / 56.0,
    10.0 / 189.0,
    -1.0 / 112.0,
    2.0 / 1925.0,
    -1.0 / 16632.0,
)
CENTER = 1.0
HALF_WIDTH = 5.0


def extended_2(block, sides, width):
    for axis, dim in sides:
        count = lax.axis_size(axis)
        forward = [(i, i + 1) for i in range(count - 1)]
        forward.append((count - 1, 0))
        backward = [(target, source) for source, target in forward]
        low = lax.ppermute(
            lax.slice_in_dim(block, block.shape[dim] - width, None, axis=dim), axis, forward
        )
        high = lax.ppermute(lax.slice_in_dim(block, 0, width, axis=dim), axis, backward)
        block = jnp.concatenate([low, block, high], axis=dim)
    return block


def exact_dot(left, right):
    return jnp.dot(left, right, precision=lax.Precision.HIGHEST, preferred_element_type=jnp.float32)


def per_device(previous, current, potential, projectors, couplings, pattern, counts, panels):
    blocks, rows_y, rows_z, width_x = current.shape
    cell_count = rows_y * rows_z * width_x
    extended = extended_2(current, (("gy", 1), ("gz", 2)), 6)
    laplacian = 3.0 * STENCIL[0] * current
    for reach in range(1, 7):
        laplacian = laplacian + STENCIL[reach] * (
            jnp.roll(current, reach, 3)
            + jnp.roll(current, -reach, 3)
            + extended[:, 6 + reach : 6 + reach + rows_y, 6 : 6 + rows_z]
            + extended[:, 6 - reach : 6 - reach + rows_y, 6 : 6 + rows_z]
            + extended[:, 6 : 6 + rows_y, 6 + reach : 6 + reach + rows_z]
            + extended[:, 6 : 6 + rows_y, 6 - reach : 6 - reach + rows_z]
        )
    own_tile = lax.axis_index("gy") * lax.axis_size("gz") + lax.axis_index("gz")
    tile_count = pattern.shape[1]
    per_block = projectors.shape[0] // counts.shape[0]
    touched = jnp.sum(
        jnp.where(jnp.arange(tile_count)[None, :] == own_tile, pattern, 0), axis=1
    ).astype(jnp.float32)
    slot_live = (jnp.arange(per_block)[None, :] < counts[:, None]).astype(jnp.float32)
    weight = (touched[:, None] * slot_live).reshape(-1)
    flat_block = current.reshape(blocks, cell_count)
    proj_rows = projectors.reshape(projectors.shape[0], cell_count)
    partial_value = exact_dot(proj_rows, flat_block.T) * weight[:, None]
    base = (
        2.0 / HALF_WIDTH * (-0.5 * laplacian + potential * current - CENTER * current) - previous
    ).reshape(blocks, cell_count)
    own_rows = panels.reshape(panels.shape[0], cell_count)
    proj_sums = lax.psum(partial_value, ("gy", "gz"))
    projected = exact_dot(((couplings * weight)[:, None] * proj_sums).T, proj_rows)
    filtered = base + 2.0 / HALF_WIDTH * projected
    gathered = lax.all_gather(own_rows, "band", axis=0, tiled=True)
    intersection = exact_dot(gathered, filtered.T)
    coefficients = lax.psum(intersection, ("gy", "gz"))
    rotated = filtered - exact_dot(coefficients.T, gathered)
    return (rotated.reshape(blocks, rows_y, rows_z, width_x), coefficients)


def solution(mesh):
    in_specs = (
        P("band", "gy", "gz", None),
        P("band", "gy", "gz", None),
        P("gy", "gz", None),
        P(None, "gy", "gz", None),
        P(),
        P(),
        P(),
        P("band", "gy", "gz", None),
    )
    out_specs = (P("band", "gy", "gz", None), P(None, "band"))
    return jax.shard_map(
        per_device, mesh=mesh, in_specs=in_specs, out_specs=out_specs, check_vma=False
    )
```

profile of v0, /device:TPU:38, one launch (start us, length us, event | category | flops | bytes accessed | tf_op | source)
XLA Modules:
  0.0 708.4 jit_solution(8966925279136649046)
XLA Ops:
  7.2 2.9 copy.95
  10.3 2.6 collective-permute-start.1
  13.1 4.5 collective-permute-start
  20.3 1.1 copy.73
  22.5 1.1 copy.75
  23.6 1.1 copy.76
  25.8 1.1 copy.78
  28.0 1.1 copy.80
  29.1 1.1 copy.81
  34.6 1.1 copy.86
  37.9 1.1 copy.89
  40.4 1.1 copy.91
  42.0 1.6 fusion.55
  43.6 7.9 %collective-permute-start.2 = (f32[16,20,6,128]{3,0,2,1:T(8,128)}, f32[16,20,6,128]{3,0,2,1:T(8,128)}, u32[]{:S(2)}, u32[]{:S(2)}) collective-permute-start(f32[16,20,6,128]{3,0,2,1:T(8,128)} %get-tuple-element.2), channel_id=1, source_target_pairs={{8,0},{16,8},{24,16},{0,24},{9,1},{17,9},{25,17},{1,25},{10,2},{18... | collective-permute-start | bytes 2949128 | tf_op jit(solution)/shard_map/ppermute | solution.py:28
  51.5 2.1 collective-permute-start.3
  55.0 1.2 copy.93
  56.1 1.2 copy.94
  57.6 4.7 fusion.9
  62.3 319.1 %psum.14 = f32[64,16]{1,0:T(8,128)S(1)} all-reduce(f32[64,16]{1,0:T(8,128)S(1)} %fusion.9), channel_id=1, replica_groups=mesh['gy'=16,'gz'=4,'band'=8] {'gy','gz'}, use_global_device_ids=true, to_apply=%region_1.2 | all-reduce | flops 1024 | bytes 8192 | tf_op jit(solution)/shard_map/psum | solution.py:66
  381.4 8.6 %fusion.21 = f32[16,8,8,128]{3,0,2,1:T(8,128)S(1)} fusion(f32[16,20,8,128]{3,0,2,1:T(8,128)} %copy-done.1, f32[16,20,6,128]{3,0,2,1:T(8,128)} %collective-permute-done.3, f32[16,20,6,128]{3,0,2,1:T(8,128)} %collective-permute-done.2, f32[16,14,8,128]{3,0,2,1:T(8,128)S(1)} %get-tuple-element.29, f32[16,14,8,128]{3,0,2,1:T(8,128)S(1)} %get-tuple-element.33, ...), kind=kLoop, calls=%fused_computation.41 | loop fusion | flops 9568256 | bytes 17465344 | tf_op jit(solution)/shard_map/sub | solution.py:63
  390.1 2.5 fusion
  392.6 8.9 %convolution_bitcast_fusion = f32[256,16]{0,1:T(8,128)S(1)} fusion(f32[16,8192]{1,0:T(8,128)S(1)} %fusion, f32[256,8192]{1,0:T(8,128)} %all-gather.2.cloned.1.call-done), kind=kOutput, calls=%fused_computation.30 | convolution fusion | flops 402653184 | bytes 8929280 | tf_op jit(solution)/shard_map/dot_general | solution.py:34
  401.5 292.8 %psum.15 = f32[256,16]{0,1:T(8,128)S(1)} all-reduce(f32[256,16]{0,1:T(8,128)S(1)} %convolution_bitcast_fusion), channel_id=1, replica_groups=mesh['gy'=16,'gz'=4,'band'=8] {'gy','gz'}, use_global_device_ids=true, to_apply=%region_2.3 | all-reduce | flops 4096 | bytes 32768 | tf_op jit(solution)/shard_map/psum | solution.py:71
  694.3 6.4 fusion.5
  (62 shorter events, 17.5 us)
Async XLA Ops:
  7.2 3.0 copy-start
  7.2 385.5 %all-gather.2.cloned.1.call-start = ((), (), s32[]{:S(2)}) async-start(), calls=%async_computation | async-start | bytes 9437184 | tf_op jit(solution)/shard_map/all_gather | solution.py:69
  10.3 31.1 %collective-permute-start.1 = (f32[16,6,8,128]{3,0,2,1:T(8,128)S(1)}, f32[16,6,8,128]{3,0,2,1:T(8,128)S(1)}, u32[]{:S(2)}, u32[]{:S(2)}) collective-permute-start(f32[16,6,8,128]{3,0,2,1:T(8,128)S(1)} %copy.69), channel_id=1, source_target_pairs={{0,32},{32,64},{64,96},{96,128},{128,160},{160,192},{192,224},{224... | collective-permute-start | bytes 1179656 | tf_op jit(solution)/shard_map/ppermute | solution.py:25
  13.1 28.8 %collective-permute-start = (f32[16,6,8,128]{3,0,2,1:T(8,128)S(1)}, f32[16,6,8,128]{3,0,2,1:T(8,128)S(1)}, u32[]{:S(2)}, u32[]{:S(2)}) collective-permute-start(f32[16,6,8,128]{3,0,2,1:T(8,128)S(1)} %copy.70), channel_id=1, source_target_pairs={{32,0},{64,32},{96,64},{128,96},{160,128},{192,160},{224,192},{256... | collective-permute-start | bytes 1179656 | tf_op jit(solution)/shard_map/ppermute | solution.py:28
  42.0 11.9 %copy-start.1 = (f32[16,20,8,128]{3,0,2,1:T(8,128)}, f32[16,20,8,128]{3,0,2,1:T(8,128)S(1)}, u32[]{:S(2)}) copy-start(f32[16,20,8,128]{3,0,2,1:T(8,128)S(1)} %get-tuple-element.34) | copy-start | bytes 3932164
  43.6 337.8 %collective-permute-start.2 = (f32[16,20,6,128]{3,0,2,1:T(8,128)}, f32[16,20,6,128]{3,0,2,1:T(8,128)}, u32[]{:S(2)}, u32[]{:S(2)}) collective-permute-start(f32[16,20,6,128]{3,0,2,1:T(8,128)} %get-tuple-element.2), channel_id=1, source_target_pairs={{8,0},{16,8},{24,16},{0,24},{9,1},{17,9},{25,17},{1,25},{10,2},{18... | collective-permute-start | bytes 2949128 | tf_op jit(solution)/shard_map/ppermute | solution.py:28
  51.5 329.9 %collective-permute-start.3 = (f32[16,20,6,128]{3,0,2,1:T(8,128)}, f32[16,20,6,128]{3,0,2,1:T(8,128)}, u32[]{:S(2)}, u32[]{:S(2)}) collective-permute-start(f32[16,20,6,128]{3,0,2,1:T(8,128)} %get-tuple-element.3), channel_id=1, source_target_pairs={{0,8},{8,16},{16,24},{24,0},{1,9},{9,17},{17,25},{25,1},{2,10},{10... | collective-permute-start | bytes 2949128 | tf_op jit(solution)/shard_map/ppermute | solution.py:25
  53.8 3.5 copy-start.5
  53.8 3.6 copy-start.6
  53.9 3.7 copy-start.7
  56.1 325.3 %copy-start.4 = (f32[8,8,128]{2,1,0:T(8,128)S(1)}, f32[8,8,128]{2,1,0:T(8,128)}, u32[]{:S(2)}) copy-start(f32[8,8,128]{2,1,0:T(8,128)} %param.10) | copy-start | bytes 98308
  381.4 8.8 %copy-start.2 = (f32[64,8,8,128]{3,2,1,0:T(8,128)S(1)}, f32[64,8,8,128]{3,2,1,0:T(8,128)}, u32[]{:S(2)}) copy-start(f32[64,8,8,128]{3,2,1,0:T(8,128)} %param.11) | copy-start | bytes 6291460
  694.3 6.4 copy-start.3
Sparse Core Ops, SparseCore 0:
  10.2 57.5 all-gather.1
where the time goes:
time: 709 us; the launch traced here: 708 us
  blocking collectives  612 us (86%)
  local copies, waits for them, and re-layouts  34 us (5%)
  matrix products  22.4 us (3%)
  starting transfers between devices  17.1 us (2%)
  between operations  14.3 us (2%)
  other arithmetic  8.76 us (1%)
    psum x1, blocking collectives, per_device(): proj_sums = lax.psum(partial_value, ('gy', 'gz'))  319 us
    psum x1, blocking collectives, per_device(): coefficients = lax.psum(intersection, ('gy', 'gz'))  293 us
    unnamed x46, local copies, waits for them, and re-layouts  29.4 us
    dot_general x4, matrix products, exact_dot(): jnp.dot(left, right, precision=lax.Precision.HIGHEST, preferred_element_t...  22.4 us
  transfers between devices with their start and end apart: 5, of which 0 were waited for; matrix products, arithmetic and copies ran while one was open for 7% of the time, Pallas kernels for 0%

commit v1 on v0

--- a/solution.py
+++ b/solution.py
@@ -63,7 +63,7 @@
         2.0 / HALF_WIDTH * (-0.5 * laplacian + potential * current - CENTER * current) - previous
     ).reshape(blocks, cell_count)
     own_rows = panels.reshape(panels.shape[0], cell_count)
-    proj_sums = lax.psum(partial_value, ("gy", "gz"))
+    proj_sums = lax.psum(lax.psum(partial_value, "gy"), "gz")
     projected = exact_dot(((couplings * weight)[:, None] * proj_sums).T, proj_rows)
     filtered = base + 2.0 / HALF_WIDTH * projected
     gathered = lax.all_gather(own_rows, "band", axis=0, tiled=True)

time: 709 us -> 495 us (0.70)
  the two profiles are of different devices: /device:TPU:38 before, /device:TPU:32 now
where the time goes in v1:
time: 495 us
  blocking collectives  398 us (80%)
  local copies, waits for them, and re-layouts  34.1 us (7%)
  matrix products  22.4 us (5%)
  starting transfers between devices  17.1 us (3%)
  between operations  14.3 us (3%)
  other arithmetic  8.86 us (2%)
    psum x1, blocking collectives, per_device(): coefficients = lax.psum(intersection, ('gy', 'gz'))  293 us
    psum x2, blocking collectives, per_device(): proj_sums = lax.psum(lax.psum(partial_value, 'gy'), 'gz')  105 us
    unnamed x46, local copies, waits for them, and re-layouts  29.6 us
    dot_general x4, matrix products, exact_dot(): jnp.dot(left, right, precision=lax.Precision.HIGHEST, preferred_element_t...  22.4 us
    ppermute x2, starting transfers between devices, extended_2(): lax.ppermute(lax.slice_in_dim(block, 0, width, axis=dim), axis, backward)  12.4 us
  transfers between devices with their start and end apart: 5, of which 0 were waited for; matrix products, arithmetic and copies ran while one was open for 9% of the time, Pallas kernels for 0%

profile of v1, /device:TPU:32, one launch (start us, length us, event | category | flops | bytes accessed | tf_op | source)
XLA Modules:
  0.0 494.6 jit_solution(3829596109721323229)
XLA Ops:
  7.2 2.9 copy.95
  10.3 2.6 collective-permute-start.1
  13.1 4.5 collective-permute-start
  22.5 1.1 copy.75
  24.7 1.1 copy.77
  28.1 1.1 copy.80
  29.2 1.1 copy.81
  36.9 1.1 copy.88
  38.0 1.1 copy.89
  40.5 1.1 copy.91
  42.1 1.6 fusion.55
  43.7 7.9 %collective-permute-start.2 = (f32[16,20,6,128]{3,0,2,1:T(8,128)}, f32[16,20,6,128]{3,0,2,1:T(8,128)}, u32[]{:S(2)}, u32[]{:S(2)}) collective-permute-start(f32[16,20,6,128]{3,0,2,1:T(8,128)} %get-tuple-element.2), channel_id=1, source_target_pairs={{8,0},{16,8},{24,16},{0,24},{9,1},{17,9},{25,17},{1,25},{10,2},{18... | collective-permute-start | bytes 2949128 | tf_op jit(solution)/shard_map/ppermute | solution.py:28
  51.6 2.1 collective-permute-start.3
  54.0 1.1 copy.92
  55.1 1.1 copy.93
  56.2 1.2 copy.94
  57.7 4.7 fusion.9
  62.4 85.3 %psum.21 = f32[64,16]{1,0:T(8,128)S(1)} all-reduce(f32[64,16]{1,0:T(8,128)S(1)} %fusion.9), channel_id=1, replica_groups=mesh['gy'=16,'gz'=4,'band'=8] {'gy'}, use_global_device_ids=true, to_apply=%region_1.2 | all-reduce | flops 1024 | bytes 8192 | tf_op jit(solution)/shard_map/psum | solution.py:66
  147.7 19.7 %psum.22 = f32[64,16]{1,0:T(8,128)S(1)} all-reduce(f32[64,16]{1,0:T(8,128)S(1)} %psum.21), channel_id=1, replica_groups=mesh['gy'=16,'gz'=4,'band'=8] {'gz'}, use_global_device_ids=true, to_apply=%region_2.3 | all-reduce | flops 1024 | bytes 8192 | tf_op jit(solution)/shard_map/psum | solution.py:66
  167.5 8.7 %fusion.21 = f32[16,8,8,128]{3,0,2,1:T(8,128)S(1)} fusion(f32[16,20,8,128]{3,0,2,1:T(8,128)} %copy-done.1, f32[16,20,6,128]{3,0,2,1:T(8,128)} %collective-permute-done.3, f32[16,20,6,128]{3,0,2,1:T(8,128)} %collective-permute-done.2, f32[16,14,8,128]{3,0,2,1:T(8,128)S(1)} %get-tuple-element.29, f32[16,14,8,128]{3,0,2,1:T(8,128)S(1)} %get-tuple-element.33, ...), kind=kLoop, calls=%fused_computation.41 | loop fusion | flops 9568256 | bytes 17465344 | tf_op jit(solution)/shard_map/sub | solution.py:63
  176.3 2.5 fusion
  178.8 8.9 %convolution_bitcast_fusion = f32[256,16]{0,1:T(8,128)S(1)} fusion(f32[16,8192]{1,0:T(8,128)S(1)} %fusion, f32[256,8192]{1,0:T(8,128)} %all-gather.2.cloned.1.call-done), kind=kOutput, calls=%fused_computation.30 | convolution fusion | flops 402653184 | bytes 8929280 | tf_op jit(solution)/shard_map/dot_general | solution.py:34
  187.7 292.8 %psum.23 = f32[256,16]{0,1:T(8,128)S(1)} all-reduce(f32[256,16]{0,1:T(8,128)S(1)} %convolution_bitcast_fusion), channel_id=1, replica_groups=mesh['gy'=16,'gz'=4,'band'=8] {'gy','gz'}, use_global_device_ids=true, to_apply=%region_3.4 | all-reduce | flops 4096 | bytes 32768 | tf_op jit(solution)/shard_map/psum | solution.py:71
  480.5 6.4 %fusion.5 = f32[2,8,64,128]{3,1,2,0:T(8,128)S(1)} fusion(f32[16,8192]{1,0:T(8,128)S(1)} %fusion, f32[256,16]{0,1:T(8,128)S(1)} %psum.23, f32[256,8192]{1,0:T(8,128)} %all-gather.2.cloned.1.call-done), kind=kOutput, calls=%fused_computation.27 | convolution fusion | flops 402784256 | bytes 9453568 | tf_op jit(solution)/shard_map/dot_general | solution.py:34
  (63 shorter events, 18.6 us)
Async XLA Ops:
  7.2 3.0 copy-start
  7.2 171.6 %all-gather.2.cloned.1.call-start = ((), (), s32[]{:S(2)}) async-start(), calls=%async_computation | async-start | bytes 9437184 | tf_op jit(solution)/shard_map/all_gather | solution.py:69
  10.3 31.2 %collective-permute-start.1 = (f32[16,6,8,128]{3,0,2,1:T(8,128)S(1)}, f32[16,6,8,128]{3,0,2,1:T(8,128)S(1)}, u32[]{:S(2)}, u32[]{:S(2)}) collective-permute-start(f32[16,6,8,128]{3,0,2,1:T(8,128)S(1)} %copy.69), channel_id=1, source_target_pairs={{0,32},{32,64},{64,96},{96,128},{128,160},{160,192},{192,224},{224... | collective-permute-start | bytes 1179656 | tf_op jit(solution)/shard_map/ppermute | solution.py:25
  13.1 28.9 %collective-permute-start = (f32[16,6,8,128]{3,0,2,1:T(8,128)S(1)}, f32[16,6,8,128]{3,0,2,1:T(8,128)S(1)}, u32[]{:S(2)}, u32[]{:S(2)}) collective-permute-start(f32[16,6,8,128]{3,0,2,1:T(8,128)S(1)} %copy.70), channel_id=1, source_target_pairs={{32,0},{64,32},{96,64},{128,96},{160,128},{192,160},{224,192},{256... | collective-permute-start | bytes 1179656 | tf_op jit(solution)/shard_map/ppermute | solution.py:28
  42.1 11.9 %copy-start.1 = (f32[16,20,8,128]{3,0,2,1:T(8,128)}, f32[16,20,8,128]{3,0,2,1:T(8,128)S(1)}, u32[]{:S(2)}) copy-start(f32[16,20,8,128]{3,0,2,1:T(8,128)S(1)} %get-tuple-element.34) | copy-start | bytes 3932164
  43.7 123.7 %collective-permute-start.2 = (f32[16,20,6,128]{3,0,2,1:T(8,128)}, f32[16,20,6,128]{3,0,2,1:T(8,128)}, u32[]{:S(2)}, u32[]{:S(2)}) collective-permute-start(f32[16,20,6,128]{3,0,2,1:T(8,128)} %get-tuple-element.2), channel_id=1, source_target_pairs={{8,0},{16,8},{24,16},{0,24},{9,1},{17,9},{25,17},{1,25},{10,2},{18... | collective-permute-start | bytes 2949128 | tf_op jit(solution)/shard_map/ppermute | solution.py:28
  51.6 115.8 %collective-permute-start.3 = (f32[16,20,6,128]{3,0,2,1:T(8,128)}, f32[16,20,6,128]{3,0,2,1:T(8,128)}, u32[]{:S(2)}, u32[]{:S(2)}) collective-permute-start(f32[16,20,6,128]{3,0,2,1:T(8,128)} %get-tuple-element.3), channel_id=1, source_target_pairs={{0,8},{8,16},{16,24},{24,0},{1,9},{9,17},{17,25},{25,1},{2,10},{10... | collective-permute-start | bytes 2949128 | tf_op jit(solution)/shard_map/ppermute | solution.py:25
  53.9 3.5 copy-start.5
  53.9 3.6 copy-start.6
  54.0 3.7 copy-start.7
  56.2 111.2 %copy-start.4 = (f32[8,8,128]{2,1,0:T(8,128)S(1)}, f32[8,8,128]{2,1,0:T(8,128)}, u32[]{:S(2)}) copy-start(f32[8,8,128]{2,1,0:T(8,128)} %param.10) | copy-start | bytes 98308
  167.4 8.9 %copy-start.2 = (f32[64,8,8,128]{3,2,1,0:T(8,128)S(1)}, f32[64,8,8,128]{3,2,1,0:T(8,128)}, u32[]{:S(2)}) copy-start(f32[64,8,8,128]{3,2,1,0:T(8,128)} %param.11) | copy-start | bytes 6291460
  480.5 6.4 %copy-start.3 = (f32[256,16]{0,1:T(8,128)}, f32[256,16]{0,1:T(8,128)S(1)}, u32[]{:S(2)}) copy-start(f32[256,16]{0,1:T(8,128)S(1)} %psum.23) | copy-start | bytes 49156
Sparse Core Ops, SparseCore 0:
  10.2 59.3 all-gather.1
